TPU v7x, 32 devices: a whole 2x2x4 slice. The times are simulated.
32 devices in a mesh: groups: 2 (over y), ctx: 4 (over z), exp: 2 (over x), tp: 2 (over core).
Axes of the slice: x: 2, y: 2, z: 4, core: 2. Of those that a mesh axis runs over, the one named last changes fastest.
Arguments:
- tokens: bfloat16 [4096, 6144], P(('groups', 'ctx', 'tp'), 'exp'), parts along dimension 0, may hold values from -6 to 6
- cotangent: bfloat16 [4096, 6144], P(('groups', 'ctx', 'tp'), 'exp'), parts along dimension 0, may hold values from -6 to 6
- route_logits: float32 [4096, 2], P(('groups', 'ctx', 'tp')), parts along dimension 0, may hold values from -6 to 6
- expert_ids: int32 [4096, 2], P(('groups', 'ctx', 'tp')), parts along dimension 0, may hold values from 0 to 7, as said below
- w_gate: bfloat16 [8192, 6144], P(('ctx', 'tp'), 'exp'), may hold values from -0.078125 to 0.078125
- w_up: bfloat16 [8192, 6144], P(('ctx', 'tp'), 'exp'), may hold values from -0.078125 to 0.078125
- w_down: bfloat16 [8192, 6144], P(('ctx', 'tp'), 'exp'), may hold values from -0.0625 to 0.0625
Outputs:
- token_grad: bfloat16 [4096, 6144], P(('groups', 'ctx', 'tp'), 'exp'), parts along dimension 0
- logit_grad: float32 [4096, 2], P(('groups', 'ctx', 'tp')), parts along dimension 0
- gate_grad: bfloat16 [16384, 6144], P(('groups', 'ctx', 'tp'), 'exp'), parts along dimension 0
- up_grad: bfloat16 [16384, 6144], P(('groups', 'ctx', 'tp'), 'exp'), parts along dimension 0
- down_grad: bfloat16 [16384, 6144], P(('groups', 'ctx', 'tp'), 'exp'), parts along dimension 0
There are 2 independent parts, one for each index of `groups`. A program takes and returns all parts, laid end to end along the dimension named above; an argument that names none is the same for every part. Nothing has to cross between parts.
Inputs may be any that keep to these rules, and one draw needn't show every extreme that they name: `expert_ids`: the two experts of a token differ. In each aligned block of 256 rows (the rows of one device) at most 32 rows name expert 0, and in every draw some block has exactly 32 such rows.
All inputs are finite; a program needn't handle non-finite values.
Results may differ from a plain program's by a relative error of at most 0.013.
Values may be sent and summed in bfloat16 or wider, within the bound.
A program may use at most 128 MiB of HBM per device.

v0:
```python
import jax
import jax.numpy as jnp
from jax import lax
from jax.sharding import PartitionSpec as P

CAP = 32


def route_weights(route_logits):
    first = jax.nn.sigmoid(route_logits[:, 0] - route_logits[:, 1])
    second = jax.nn.sigmoid(route_logits[:, 1] - route_logits[:, 0])
    return jnp.stack([first, second], axis=1)


def contract_rows(left, right):
    return lax.dot_general(
        left, right, (((1,), (1,)), ((), ())), preferred_element_type=jnp.float32
    )


def contract_slots(left, right):
    return lax.dot_general(
        left, right, (((0,), (0,)), ((), ())), preferred_element_type=jnp.float32
    )


def slot_math(gate_pre, up_pre, back, share_bf):
    share_f = share_bf.astype(jnp.float32)[:, None]
    sig_gate = jax.nn.sigmoid(gate_pre)
    activated = gate_pre * sig_gate
    hidden = (activated * up_pre).astype(jnp.bfloat16)
    weighted = (share_f * hidden.astype(jnp.float32)).astype(jnp.bfloat16)
    score_local = jnp.sum(hidden.astype(jnp.float32) * back, axis=1)
    hidden_back = share_f * back
    gate_back = (hidden_back * up_pre * sig_gate * (1.0 + gate_pre * (1.0 - sig_gate))).astype(
        jnp.bfloat16
    )
    up_back = (hidden_back * activated).astype(jnp.bfloat16)
    return (gate_back, up_back, weighted, score_local)


def shards(tokens, cotangent, route_logits, expert_ids, w_gate, w_up, w_down):
    row_count, feature_part = tokens.shape
    hit_mask = expert_ids == 0
    chosen = jnp.any(hit_mask, axis=1)
    chosen_int = chosen.astype(jnp.int32)
    position = jnp.cumsum(chosen_int) - chosen_int
    target = jnp.where(chosen, position, CAP)
    shares = route_weights(route_logits)
    token_share = jnp.sum(jnp.where(hit_mask, shares, 0.0), axis=1).astype(jnp.bfloat16)
    x_send = jnp.zeros((CAP, feature_part), jnp.bfloat16).at[target].set(tokens, mode="drop")
    dy_send = jnp.zeros((CAP, feature_part), jnp.bfloat16).at[target].set(cotangent, mode="drop")
    share_send = jnp.zeros((CAP,), jnp.bfloat16).at[target].set(token_share, mode="drop")
    x_all, dy_all, share_all = (
        lax.all_gather(x_send, ("ctx", "tp"), axis=0, tiled=True),
        lax.all_gather(dy_send, ("ctx", "tp"), axis=0, tiled=True),
        lax.all_gather(share_send, ("ctx", "tp"), axis=0, tiled=True),
    )
    partials = (
        contract_rows(x_all, w_gate),
        contract_rows(x_all, w_up),
        contract_rows(dy_all, w_down),
    )
    gate_pre, up_pre, back = lax.psum((partials[0], partials[1], partials[2]), "exp")
    gate_back, up_back, weighted, score_part = slot_math(gate_pre, up_pre, back, share_all)
    own_score = lax.psum_scatter(score_part, ("ctx", "tp"), scatter_dimension=0, tiled=True)
    slot_grad = lax.psum_scatter(
        jnp.dot(gate_back, w_gate, preferred_element_type=jnp.float32)
        + jnp.dot(up_back, w_up, preferred_element_type=jnp.float32),
        ("ctx", "tp"),
        scatter_dimension=0,
        tiled=True,
    ).astype(jnp.bfloat16)
    source_row = jnp.where(chosen, position, 0)
    token_grad = jnp.where(chosen[:, None], slot_grad[source_row], jnp.zeros((), jnp.bfloat16))
    token_score = jnp.where(chosen, own_score[source_row], 0.0)
    score_terms = jnp.where(hit_mask, token_score[:, None], 0.0)
    mean_score = jnp.sum(shares * score_terms, axis=1, keepdims=True)
    logit_grad = shares * (score_terms - mean_score)
    gate_grad = contract_slots(gate_back, x_all).astype(jnp.bfloat16)
    up_grad = contract_slots(up_back, x_all).astype(jnp.bfloat16)
    down_grad = contract_slots(weighted, dy_all).astype(jnp.bfloat16)
    return (token_grad, logit_grad, gate_grad, up_grad, down_grad)


def solution(mesh):
    in_specs = (
        P(("groups", "ctx", "tp"), "exp"),
        P(("groups", "ctx", "tp"), "exp"),
        P(("groups", "ctx", "tp"), None),
        P(("groups", "ctx", "tp"), None),
        P(("ctx", "tp"), "exp"),
        P(("ctx", "tp"), "exp"),
        P(("ctx", "tp"), "exp"),
    )
    out_specs = (
        P(("groups", "ctx", "tp"), "exp"),
        P(("groups", "ctx", "tp"), None),
        P(("groups", "ctx", "tp"), "exp"),
        P(("groups", "ctx", "tp"), "exp"),
        P(("groups", "ctx", "tp"), "exp"),
    )
    return jax.shard_map(shards, mesh=mesh, in_specs=in_specs, out_specs=out_specs, check_vma=False)
```

profile of v0, /device:TPU:0, one launch (start us, length us, event | category | flops | bytes accessed | tf_op | source)
XLA Modules:
  0.0 275.5 jit_solution(8475590525800658984)
XLA Ops:
  7.2 0.7 fusion.15
  7.9 0.3 reduce-window.9
  8.3 0.1 slice_reduce_fusion
  8.5 4.1 %scatter_custom_fusion.2 = bf16[32,3072]{1,0:T(8,128)(2,1)} fusion(s32[256]{0:T(256)S(1)} %bitcast.62, bf16[256,3072]{1,0:T(8,128)(2,1)} %param.7, bf16[]{:T(256)} %constant.8.clone.1), kind=kCustom, calls=%fused_computation.19 | custom fusion | bytes 197120 | tf_op jit(solution)/shard_map/scatter | solution.py:51
  12.7 4.1 %scatter_custom_fusion.1 = bf16[32,3072]{1,0:T(8,128)(2,1)} fusion(s32[256]{0:T(256)S(1)} %bitcast.63, bf16[256,3072]{1,0:T(8,128)(2,1)} %param.8, bf16[]{:T(256)} %constant.8.clone.1), kind=kCustom, calls=%fused_computation.21 | custom fusion | bytes 197120 | tf_op jit(solution)/shard_map/scatter | solution.py:52
  16.9 23.7 %all-gather.5.cloned.1.call-done = bf16[256,3072]{1,0:T(8,128)(2,1)} async-done(((bf16[32,3072]{1,0:T(8,128)(2,1)}), bf16[256,3072]{1,0:T(8,128)(2,1)}) %all-gather.5.cloned.1.call-update) | async-done | bytes 1572880 | tf_op jit(solution)/shard_map/all_gather | solution.py:55
  40.6 6.2 %fusion.21 = f32[256,1024]{1,0:T(8,128)} fusion(bf16[256,3072]{1,0:T(8,128)(2,1)} %all-gather.5.cloned.1.call-done, bf16[1024,3072]{1,0:T(8,128)(2,1)} %param.11), kind=kOutput, calls=%fused_computation.82 | convolution fusion | flops 1610612736 | bytes 8912896 | tf_op jit(solution)/shard_map/dot_general | solution.py:16
  46.8 5.6 %fusion.20 = f32[256,1024]{1,0:T(8,128)} fusion(bf16[256,3072]{1,0:T(8,128)(2,1)S(1)} %copy-done, bf16[1024,3072]{1,0:T(8,128)(2,1)} %param.12), kind=kOutput, calls=%fused_computation.81 | convolution fusion | flops 1610612736 | bytes 8912896 | tf_op jit(solution)/shard_map/dot_general | solution.py:16
  52.4 15.0 %all-gather.3.cloned.1.call-done = bf16[256,3072]{1,0:T(8,128)(2,1)} async-done(((bf16[32,3072]{1,0:T(8,128)(2,1)}), bf16[256,3072]{1,0:T(8,128)(2,1)}) %all-gather.3.cloned.1.call-update) | async-done | bytes 1572880 | tf_op jit(solution)/shard_map/all_gather | solution.py:56
  67.4 6.1 %fusion.19 = f32[256,1024]{1,0:T(8,128)} fusion(bf16[256,3072]{1,0:T(8,128)(2,1)} %all-gather.3.cloned.1.call-done, bf16[1024,3072]{1,0:T(8,128)(2,1)} %param.13), kind=kOutput, calls=%fused_computation.80 | convolution fusion | flops 1610612736 | bytes 8912896 | tf_op jit(solution)/shard_map/dot_general | solution.py:16
  73.6 0.6 copy-done.6
  74.1 0.6 fusion.16
  76.1 83.3 %all-reduce.5.cloned.1.call-done = (f32[256,1024]{1,0:T(8,128)}, f32[256,1024]{1,0:T(8,128)}, f32[256,1024]{1,0:T(8,128)}) async-done(((f32[256,1024]{1,0:T(8,128)}, f32[256,1024]{1,0:T(8,128)}, f32[256,1024]{1,0:T(8,128)}), (f32[256,1024]{1,0:T(8,128)}, f32[256,1024]{1,0:T(8,128)}, f32[256,1024]{1,0:T(8,128)})) %all-reduce.5.cloned.1.call-update) | async-done | bytes 3145744 | tf_op jit(solution)/shard_map/psum | solution.py:64
  159.3 3.1 %fusion = (f32[256]{0:T(256)S(1)}, bf16[256,1024]{1,0:T(8,128)(2,1)}) fusion(f32[256,1024]{1,0:T(8,128)} %get-tuple-element.9, f32[256,1024]{1,0:T(8,128)} %get-tuple-element.8, f32[256,1024]{1,0:T(8,128)} %get-tuple-element.7), kind=kLoop, calls=%fused_computation.11 | loop fusion | flops 2359040 | bytes 3671040 | tf_op jit(solution)/shard_map/reduce_sum | solution.py:33
  162.4 16.5 %all-reduce.1 = f32[256]{0:T(256)S(1)} all-reduce(f32[256]{0:T(256)S(1)} %get-tuple-element.10), channel_id=3, replica_groups=mesh['groups'=2,'ctx'=4,'exp'=2,'tp'=2] {'ctx','tp'}, use_global_device_ids=true, to_apply=%region_12.13.clone | all-reduce | flops 256 | bytes 2048
  179.0 0.7 fusion.18
  179.7 0.7 fusion.17
  180.4 20.1 %fusion.11 = f32[256]{0:T(256)S(1)} fusion(pred[256]{0:T(512)(128)(4,1)S(1)} %get-tuple-element.12, s32[256]{0:T(256)S(1)} %bitcast.59, f32[]{:T(128)} %bitcast.5, f32[]{:T(128)} %bitcast.6, f32[]{:T(128)} %bitcast.7, f32[]{:T(128)} %bitcast.8, f32[]{:T(128)} %bitcast.9, f32[]{:T(128)} %bitcast.10, f32[]{:T(128)} %bitcast.11, f32[]{:T(128)} %bitcast.12, ...), kind=kLoop, calls=%fused_computation.66 | loop fusion | flops 16128 | bytes 2432 | tf_op jit(solution)/shard_map/jit(_where)/select_n | solution.py:76
  200.6 2.2 scatter_custom_fusion
  202.7 0.2 dynamic-update-slice
  203.0 13.6 %all-reduce = bf16[256]{0:T(256)(128)(2,1)S(1)} all-reduce(bf16[256]{0:T(256)(128)(2,1)S(1)} %dynamic-update-slice), channel_id=1, replica_groups=mesh['groups'=2,'ctx'=4,'exp'=2,'tp'=2] {'ctx','tp'}, use_global_device_ids=true, to_apply=%add | all-reduce | flops 256 | bytes 1024
  216.6 2.3 multiply_convert_fusion.1
  218.9 4.8 %fusion.22 = f32[256,3072]{1,0:T(8,128)S(1)} fusion(bf16[256,1024]{1,0:T(8,128)(2,1)S(1)} %get-tuple-element.15, bf16[1024,3072]{1,0:T(8,128)(2,1)} %param.11), kind=kOutput, calls=%fused_computation.83 | convolution fusion | flops 1610612736 | bytes 9961472 | tf_op jit(solution)/shard_map/dot_general | solution.py:68
  223.8 3.5 %convolution_add_fusion = f32[256,3072]{1,0:T(8,128)} fusion(f32[256,3072]{1,0:T(8,128)S(1)} %fusion.22, bf16[256,1024]{1,0:T(8,128)(2,1)S(1)} %get-tuple-element.14, bf16[1024,3072]{1,0:T(8,128)(2,1)S(1)} %bitcast.58), kind=kOutput, calls=%fused_computation.7 | convolution fusion | flops 1611399168 | bytes 13107200 | tf_op jit(solution)/shard_map/dot_general | solution.py:69
  227.4 0.6 fusion.10
  228.0 4.5 %convolution_convert_fusion.1 = bf16[1024,3072]{1,0:T(8,128)(2,1)} fusion(bf16[256,1024]{1,0:T(8,128)(2,1)S(1)} %get-tuple-element.14, bf16[256,3072]{1,0:T(8,128)(2,1)S(1)} %copy-done), kind=kOutput, calls=%fused_computation.5 | convolution fusion | flops 1613758464 | bytes 8388608 | tf_op jit(solution)/shard_map/dot_general | solution.py:22
  232.5 4.5 %convolution_convert_fusion.2 = bf16[1024,3072]{1,0:T(8,128)(2,1)} fusion(bf16[256,1024]{1,0:T(8,128)(2,1)S(1)} %copy-done.3, bf16[256,3072]{1,0:T(8,128)(2,1)S(1)} %copy-done), kind=kOutput, calls=%fused_computation.6 | convolution fusion | flops 1613758464 | bytes 8388608 | tf_op jit(solution)/shard_map/dot_general | solution.py:22
  237.1 4.6 %convolution_convert_fusion = bf16[1024,3072]{1,0:T(8,128)(2,1)} fusion(bf16[256,3072]{1,0:T(8,128)(2,1)S(1)} %copy-done.5, bf16[256,1024]{1,0:T(8,128)(2,1)S(1)} %copy-done.4, f32[256]{0:T(256)S(1)} %convert_element_type.58), kind=kOutput, calls=%fused_computation.4 | convolution fusion | flops 1614544896 | bytes 8389632 | tf_op jit(solution)/shard_map/dot_general | solution.py:22
  241.7 23.4 %reduce-scatter.2.cloned.1.call-done = f32[32,3072]{1,0:T(8,128)} async-done(((f32[256,3072]{1,0:T(8,128)}), f32[32,3072]{1,0:T(8,128)}) %reduce-scatter.2.cloned.1.call-update) | async-done | bytes 393232 | tf_op jit(solution)/shard_map/reduce_scatter | solution.py:67
  265.1 1.0 convert_element_type.61
  266.1 1.6 gather_fusion
  267.7 1.3 broadcast_select_fusion
  (39 shorter events, 0.6 us)
Async XLA Ops:
  7.2 33.4 %all-gather.5.cloned.1.call-start = ((), (), s32[]{:S(2)}) async-start(), calls=%async_computation.2 | async-start | bytes 1769472 | tf_op jit(solution)/shard_map/all_gather | solution.py:55
  12.7 54.7 %all-gather.3.cloned.1.call-start = ((), (), s32[]{:S(2)}) async-start(), calls=%async_computation.1 | async-start | bytes 1769472 | tf_op jit(solution)/shard_map/all_gather | solution.py:56
  16.9 142.5 %all-reduce.5.cloned.1.call-start = ((), (), s32[]{:S(2)}) async-start(), calls=%async_computation.4 | async-start | bytes 6291456 | tf_op jit(solution)/shard_map/psum | solution.py:64
  40.6 6.2 %copy-start = (bf16[256,3072]{1,0:T(8,128)(2,1)S(1)}, bf16[256,3072]{1,0:T(8,128)(2,1)}, u32[]{:S(2)}) copy-start(bf16[256,3072]{1,0:T(8,128)(2,1)} %all-gather.5.cloned.1.call-done) | copy-start | bytes 4718596
  73.5 0.7 copy-start.6
  73.5 2.5 copy-start.7
  73.5 191.6 %reduce-scatter.2.cloned.1.call-start = ((), (), s32[]{:S(2)}) async-start(), calls=%async_computation.3 | async-start | bytes 3538944 | tf_op jit(solution)/shard_map/reduce_scatter | solution.py:67
  159.3 57.2 %copy-start.1 = (f32[256,1024]{1,0:T(8,128)S(1)}, f32[256,1024]{1,0:T(8,128)}, u32[]{:S(2)}) copy-start(f32[256,1024]{1,0:T(8,128)} %get-tuple-element.7) | copy-start | bytes 3145732
  216.6 7.2 %slice-start = ((s8[6291456]{0:T(1024)(128)(4,1)}), s8[4194304]{0:T(1024)(128)(4,1)S(1)}, s32[]{:S(2)}) async-start(s8[6291456]{0:T(1024)(128)(4,1)} %bitcast.57), calls=%async_computation.5 | async-start | bytes 8388608
  218.9 4.8 %copy-start.2 = (bf16[256,1024]{1,0:T(8,128)(2,1)}, bf16[256,1024]{1,0:T(8,128)(2,1)S(1)}, u32[]{:S(2)}) copy-start(bf16[256,1024]{1,0:T(8,128)(2,1)S(1)} %get-tuple-element.15) | copy-start | bytes 1572868
  218.9 4.8 %slice-start.1 = ((s8[6291456]{0:T(1024)(128)(4,1)}), s8[2097152]{0:T(1024)(128)(4,1)S(1)}, s32[]{:S(2)}) async-start(s8[6291456]{0:T(1024)(128)(4,1)} %bitcast.57), calls=%async_computation.6 | async-start | bytes 4194304
  228.0 4.5 %copy-start.3 = (bf16[256,1024]{1,0:T(8,128)(2,1)S(1)}, bf16[256,1024]{1,0:T(8,128)(2,1)}, u32[]{:S(2)}) copy-start(bf16[256,1024]{1,0:T(8,128)(2,1)} %copy-done.2) | copy-start | bytes 1572868
  232.5 4.5 %copy-start.4 = (bf16[256,1024]{1,0:T(8,128)(2,1)S(1)}, bf16[256,1024]{1,0:T(8,128)(2,1)}, u32[]{:S(2)}) copy-start(bf16[256,1024]{1,0:T(8,128)(2,1)} %get-tuple-element.11) | copy-start | bytes 1572868
  232.5 4.6 %copy-start.5 = (bf16[256,3072]{1,0:T(8,128)(2,1)S(1)}, bf16[256,3072]{1,0:T(8,128)(2,1)}, u32[]{:S(2)}) copy-start(bf16[256,3072]{1,0:T(8,128)(2,1)} %all-gather.3.cloned.1.call-done) | copy-start | bytes 4718596
Sparse Core Ops, SparseCore 0:
  12.8 27.7 all-gather.4
  42.8 24.5 all-gather.2
  73.6 85.6 all-reduce.4
  227.5 37.5 reduce-scatter.1
where the time goes:
time: 276 us
  waiting for transfers between devices  145 us (53%)
  matrix products  39.9 us (14%)
  blocking collectives  30.1 us (11%)
  other arithmetic  29.6 us (11%)
  between operations  15.2 us (6%)
  local copies, waits for them, and re-layouts  15.1 us (5%)
    psum x1, waiting for transfers between devices, shards(): lax.psum((partials[0], partials[1], partials[2]), 'exp')  83.3 us
    unnamed x2, blocking collectives  30.1 us
    all_gather x1, waiting for transfers between devices, shards(): lax.all_gather(x_send, ('ctx', 'tp'), axis=0, tiled=True)  23.7 us
    reduce_scatter x1, waiting for transfers between devices, shards(): lax.psum_scatter(jnp.dot(gate_back, w_gate, preferred_element_type=jnp.fl...  23.4 us
    select_n x1, other arithmetic, shards(): token_score = jnp.where(chosen, own_score[source_row], 0.0)  20.1 us
    dot_general x3, matrix products, contract_rows(): lax.dot_general(left, right, (((1,), (1,)), ((), ())), preferred_element_...  17.9 us
    all_gather x1, waiting for transfers between devices, shards(): lax.all_gather(dy_send, ('ctx', 'tp'), axis=0, tiled=True)  15 us
    dot_general x3, matrix products, contract_slots(): lax.dot_general(left, right, (((0,), (0,)), ((), ())), preferred_element_...  13.7 us
  transfers between devices with their start and end apart: 4, of which 4 were waited for; matrix products, arithmetic and copies ran while one was open for 11% of the time, Pallas kernels for 0%

commit v1 on v0

v1 whole, which is shorter than its diff:
```python
import functools

import jax
import jax.numpy as jnp
from jax import lax
from jax.experimental import pallas as pl
from jax.experimental.pallas import tpu as pltpu
from jax.sharding import PartitionSpec as P

CAP = 32
PAIR = 2 * CAP
LANES = 128
MESH = pl.DeviceIdType.MESH
F32 = jnp.float32
BF16 = jnp.bfloat16


def dot(left, right, contract):
    return lax.dot_general(
        left, right, ((contract[:1], contract[1:]), ((), ())), preferred_element_type=F32
    )


def routing(ids_ref, logits_ref):
    tokens = ids_ref.shape[1]
    hit_0, hit_1 = ids_ref[0:1, :] == 0, ids_ref[1:2, :] == 0
    chosen = jnp.where(hit_0 | hit_1, 1.0, 0.0)
    earlier = lax.broadcasted_iota(jnp.int32, (tokens, tokens), 0) < lax.broadcasted_iota(
        jnp.int32, (tokens, tokens), 1
    )
    position = dot(
        jnp.broadcast_to(chosen, (16, tokens)).astype(BF16),
        jnp.where(earlier, 1.0, 0.0).astype(BF16),
        (1, 0),
    )[0:1, :]
    slot = lax.broadcasted_iota(jnp.int32, (CAP, tokens), 0).astype(F32)
    pick = jnp.where(slot == position, 1.0, 0.0) * chosen
    gap = logits_ref[0:1, :] - logits_ref[1:2, :]
    return pick, (hit_0, hit_1), (jax.nn.sigmoid(gap), jax.nn.sigmoid(-gap))


def split_score(score):
    high = score.astype(BF16)
    return high, (score - high.astype(F32)).astype(BF16)


def exchange_kernel(
    n, n_exp,
    ids_ref, logits_ref, tok_hbm, cot_hbm, wg_hbm, wu_hbm, wd_hbm,
    xdy_out, act_out, sg_ref, score_ref,
    tok, cot, wg, wu, wd, xdy, part, psend, precv, act, grad, sib_out, sib_in, rs_out, rs_in, acc,
    load_sem, ag_send, ag_recv, sib_send, sib_recv, x_send, x_recv,
    gs_send, gs_recv, rs_send, rs_recv, xo_sem, ao_sem,
):
    c, e, tp = lax.axis_index("ctx"), lax.axis_index("exp"), lax.axis_index("tp")
    sib = 1 - tp
    width = wg.shape[1]
    ff = wg.shape[0]
    ff_tile = min(ff, 256)
    col_tile = 512 if width % 512 == 0 else 256

    loads = [
        pltpu.make_async_copy(src, dst, load_sem.at[i])
        for i, (src, dst) in enumerate(
            ((tok_hbm, tok), (cot_hbm, cot), (wg_hbm, wg), (wu_hbm, wu), (wd_hbm, wd))
        )
    ]
    for load in loads[:2]:
        load.start()

    barrier = pltpu.get_barrier_semaphore()
    for step in range(1, n):
        pl.semaphore_signal(
            barrier, inc=1, device_id={"ctx": lax.rem(c + step, n)}, device_id_type=MESH
        )
    for step in range(1, n_exp):
        pl.semaphore_signal(
            barrier, inc=1, device_id={"exp": lax.rem(e + step, n_exp)}, device_id_type=MESH
        )
    pl.semaphore_signal(barrier, inc=1, device_id={"tp": sib}, device_id_type=MESH)

    def half(j, which):
        return pl.ds(pl.multiple_of(j * PAIR + which * CAP, CAP), CAP)

    def pair(j):
        return pl.ds(pl.multiple_of(j * PAIR, PAIR), PAIR)

    def block_half(which):
        return pl.ds(pl.multiple_of(which * CAP, CAP), CAP)

    def gather_copy(j, side):
        to = jnp.where(c + 1 < n, c + 1, 0) if side == 1 else jnp.where(c > 0, c - 1, n - 1)
        return pltpu.make_async_remote_copy(
            src_ref=xdy.at[half(j, tp)], dst_ref=xdy.at[half(j, tp)],
            send_sem=ag_send.at[j, side], recv_sem=ag_recv.at[j],
            device_id={"ctx": to}, device_id_type=MESH,
        )

    def twin_copy(j, which):
        return pltpu.make_async_remote_copy(
            src_ref=xdy.at[half(j, which)], dst_ref=xdy.at[half(j, which)],
            send_sem=sib_send.at[j], recv_sem=sib_recv.at[j],
            device_id={"tp": sib}, device_id_type=MESH,
        )

    def partial_copy(j, i, step):
        return pltpu.make_async_remote_copy(
            src_ref=psend.at[i, pair(j)], dst_ref=precv.at[step - 1, i, pair(j)],
            send_sem=x_send.at[step - 1, i, j], recv_sem=x_recv.at[step - 1, i, j],
            device_id={"exp": lax.rem(e + step, n_exp)}, device_id_type=MESH,
        )

    def pair_sum_copy(j):
        return pltpu.make_async_remote_copy(
            src_ref=sib_out.at[j], dst_ref=sib_in.at[j],
            send_sem=gs_send.at[j], recv_sem=gs_recv.at[j],
            device_id={"tp": sib}, device_id_type=MESH,
        )

    def home_copy(j, source):
        return pltpu.make_async_remote_copy(
            src_ref=rs_out.at[j], dst_ref=rs_in.at[source],
            send_sem=rs_send.at[j], recv_sem=rs_recv.at[source],
            device_id={"ctx": j}, device_id_type=MESH,
        )

    def xdy_store(j):
        return pltpu.make_async_copy(xdy.at[pair(j)], xdy_out.at[pair(j)], xo_sem.at[j])

    def act_store(j):
        return pltpu.make_async_copy(act.at[pair(j)], act_out.at[pair(j)], ao_sem.at[j])

    pick, hits, shares = routing(ids_ref, logits_ref)
    token_share = jnp.where(hits[0], shares[0], 0.0) + jnp.where(hits[1], shares[1], 0.0)
    token_share = token_share.astype(BF16).astype(F32)
    share = jnp.sum(pick * token_share, axis=1, keepdims=True)
    mine = half(c, tp)
    xdy[mine, 2 * width:] = jnp.broadcast_to(share, (CAP, LANES)).astype(BF16)
    pick = pick.astype(BF16)
    for which, ref in enumerate((tok, cot)):
        loads[which].wait()
        for at in range(0, width, col_tile):
            xdy[mine, which * width + at:which * width + at + col_tile] = dot(
                pick, ref[:, at:at + col_tile], (1, 0)
            ).astype(BF16)

    for load in loads[2:]:
        load.start()
    pl.semaphore_wait(barrier, n + n_exp - 1)

    @pl.when(c + 1 < n)
    def _():
        gather_copy(c, 1).start()

    @pl.when(c > 0)
    def _():
        gather_copy(c, 0).start()

    twin_copy(c, tp).start()

    both = jnp.where(2 * c <= n - 1, c, n - 1 - c)

    def nth(k):
        near = c + jnp.where(k % 2 == 0, 1, -1) * ((k + 1) // 2)
        far = jnp.where(2 * c <= n - 1, k, n - 1 - k)
        return jnp.where(k <= 2 * both, near, far)

    def arrive(j):
        gather_copy(j, 1).wait_recv()

        @pl.when((j < c) & (c + 1 < n))
        def _():
            gather_copy(j, 1).start()

        @pl.when((j > c) & (c > 0))
        def _():
            gather_copy(j, 0).start()

        twin_copy(j, tp).start()

    def forward(k):
        j = nth(k)
        paired = k <= 2 * both

        @pl.when((k > 0) & jnp.logical_not(paired & (k % 2 == 0)))
        def _():
            arrive(j)

        @pl.when((k % 2 == 1) & (k + 1 <= 2 * both))
        def _():
            arrive(nth(k + 1))

        twin_copy(j, sib).wait_recv()
        xdy_store(j).start()
        rows = pair(j)
        for i, (weight, first) in enumerate(((wg, 0), (wu, 0), (wd, width))):
            @pl.when(k == 0)
            def _():
                loads[2 + i].wait()

            block = xdy[rows, first:first + width]
            for at in range(0, ff, ff_tile):
                out = dot(block, weight[at:at + ff_tile, :], (1, 1))
                part[i, rows, at:at + ff_tile] = out
                psend[i, rows, at:at + ff_tile] = out.astype(BF16)
            for step in range(1, n_exp):
                partial_copy(j, i, step).start()

    def backward(k):
        j = nth(k)
        rows = pair(j)
        slot = k % 2
        for i in range(3):
            for step in range(1, n_exp):
                partial_copy(j, i, step).wait_recv()
        share = xdy[rows, 2 * width:2 * width + 1].astype(F32)
        score = jnp.zeros((PAIR, 1), F32)
        for at in range(0, ff, ff_tile):
            sums = []
            for i in range(3):
                total = part[i, rows, at:at + ff_tile]
                for step in range(1, n_exp):
                    total = total + precv[step - 1, i, rows, at:at + ff_tile].astype(F32)
                sums.append(total)
            gate_pre, up_pre, back = sums
            sig = jax.nn.sigmoid(gate_pre)
            activated = gate_pre * sig
            hidden = (activated * up_pre).astype(BF16).astype(F32)
            score = score + jnp.sum(hidden * back, axis=1, keepdims=True)
            shared = share * back
            act[rows, at:at + ff_tile] = (
                shared * up_pre * sig * (1.0 + gate_pre * (1.0 - sig))
            ).astype(BF16)
            act[rows, ff + at:ff + at + ff_tile] = (shared * activated).astype(BF16)
            act[rows, 2 * ff + at:2 * ff + at + ff_tile] = (share * hidden).astype(BF16)
        act_store(j).start()
        gate_back, up_back = act[rows, 0:ff], act[rows, ff:2 * ff]
        for at in range(0, width, col_tile):
            grad[slot, :, at:at + col_tile] = dot(gate_back, wg[:, at:at + col_tile], (1, 0)) + dot(
                up_back, wu[:, at:at + col_tile], (1, 0)
            )
        grad[slot, :, width:] = jnp.broadcast_to(score, (PAIR, LANES))

        theirs = block_half(sib)
        sib_out[j, :, 0:width] = grad[slot, theirs, 0:width].astype(BF16)
        high, low = split_score(grad[slot, theirs, width:])
        sib_out[j, :, width:width + LANES] = high
        sib_out[j, :, width + LANES:] = low
        pair_sum_copy(j).start()

    def finish(k):
        j = nth(k)
        slot, ours = k % 2, block_half(tp)
        pair_sum_copy(j).wait_recv()
        main = grad[slot, ours, 0:width] + sib_in[j, :, 0:width].astype(F32)
        total = (
            grad[slot, ours, width:]
            + sib_in[j, :, width:width + LANES].astype(F32)
            + sib_in[j, :, width + LANES:].astype(F32)
        )

        @pl.when(j == c)
        def _():
            acc[:, 0:width] = main
            acc[:, width:] = total

        @pl.when(j != c)
        def _():
            rs_out[j, :, 0:width] = main.astype(BF16)
            high, low = split_score(total)
            rs_out[j, :, width:width + LANES] = high
            rs_out[j, :, width + LANES:] = low
            home_copy(j, c).start()

    @pl.loop(0, n)
    def _(k):
        forward(k)

    @pl.loop(0, n + 1)
    def _(k):
        @pl.when(k >= 1)
        def _():
            finish(k - 1)

        @pl.when(k < n)
        def _():
            backward(k)

    @pl.loop(0, n)
    def _(j):
        @pl.when(j != c)
        def _():
            home_copy(j, j).wait_recv()
            acc[:, 0:width] += rs_in[j, :, 0:width].astype(F32)
            acc[:, width:] += rs_in[j, :, width:width + LANES].astype(F32) + rs_in[
                j, :, width + LANES:
            ].astype(F32)

    sg_ref[...] = acc[:, 0:width].astype(BF16)
    score_ref[...] = acc[:, width:]

    @pl.loop(0, n)
    def _(j):
        @pl.when((j <= c) & (c + 1 < n))
        def _():
            gather_copy(j, 1).wait_send()

        @pl.when((j >= c) & (c > 0))
        def _():
            gather_copy(j, 0).wait_send()

        twin_copy(j, tp).wait_send()
        for i in range(3):
            for step in range(1, n_exp):
                partial_copy(j, i, step).wait_send()
        pair_sum_copy(j).wait_send()

        @pl.when(j != c)
        def _():
            home_copy(j, c).wait_send()

        xdy_store(j).wait()
        act_store(j).wait()


def exchange(n, n_exp, ids, logits, tokens, cotangent, w_gate, w_up, w_down):
    rows, width = tokens.shape
    ff = w_gate.shape[0]
    slots = n * PAIR
    wide = 2 * width + LANES
    home = width + 2 * LANES
    vmem = pl.BlockSpec(memory_space=pltpu.VMEM)
    hbm = pl.BlockSpec(memory_space=pl.ANY)
    dma = pltpu.SemaphoreType.DMA
    return pl.pallas_call(
        functools.partial(exchange_kernel, n, n_exp),
        out_shape=(
            jax.ShapeDtypeStruct((slots, wide), BF16),
            jax.ShapeDtypeStruct((slots, 3 * ff), BF16),
            jax.ShapeDtypeStruct((CAP, width), BF16),
            jax.ShapeDtypeStruct((CAP, LANES), F32),
        ),
        in_specs=[vmem, vmem] + [hbm] * 5,
        out_specs=(hbm, hbm, vmem, vmem),
        scratch_shapes=[
            pltpu.VMEM((rows, width), BF16),
            pltpu.VMEM((rows, width), BF16),
            pltpu.VMEM((ff, width), BF16),
            pltpu.VMEM((ff, width), BF16),
            pltpu.VMEM((ff, width), BF16),
            pltpu.VMEM((slots, wide), BF16),
            pltpu.VMEM((3, slots, ff), F32),
            pltpu.VMEM((3, slots, ff), BF16),
            pltpu.VMEM((n_exp - 1, 3, slots, ff), BF16),
            pltpu.VMEM((slots, 3 * ff), BF16),
            pltpu.VMEM((2, PAIR, width + LANES), F32),
            pltpu.VMEM((n, CAP, home), BF16),
            pltpu.VMEM((n, CAP, home), BF16),
            pltpu.VMEM((n, CAP, home), BF16),
            pltpu.VMEM((n, CAP, home), BF16),
            pltpu.VMEM((CAP, width + LANES), F32),
            dma((5,)),
            dma((n, 2)),
            dma((n,)),
            dma((n,)),
            dma((n,)),
            dma((n_exp - 1, 3, n)),
            dma((n_exp - 1, 3, n)),
            dma((n,)),
            dma((n,)),
            dma((n,)),
            dma((n,)),
            dma((n,)),
            dma((n,)),
        ],
        compiler_params=pltpu.CompilerParams(
            collective_id=0, has_side_effects=True, vmem_limit_bytes=56 * 1024 * 1024
        ),
    )(ids, logits, tokens, cotangent, w_gate, w_up, w_down)


def grads_kernel(
    ids_ref, logits_ref, score_ref, sg_ref, act_ref, x_ref, dy_ref,
    token_grad, logit_grad, gate_grad, up_grad, down_grad, turned, pick_ref,
):
    ff = gate_grad.shape[0]

    @pl.when(pl.program_id(0) == 0)
    def _():
        pick, hits, shares = routing(ids_ref, logits_ref)
        pick_ref[...] = pick.astype(BF16)
        token_score = jnp.sum(pick * score_ref[:, 0:1], axis=0, keepdims=True)
        terms = [jnp.where(hit, token_score, 0.0) for hit in hits]
        mean = shares[0] * terms[0] + shares[1] * terms[1]
        logit_grad[0:1, :] = shares[0] * (terms[0] - mean)
        logit_grad[1:2, :] = shares[1] * (terms[1] - mean)
        for at in range(0, 3 * ff, 256):
            turned[at:at + 256, :] = act_ref[:, at:at + 256].T

    x, dy = x_ref[...], dy_ref[...]
    gate_grad[...] = dot(turned[0:ff, :], x, (1, 0)).astype(BF16)
    up_grad[...] = dot(turned[ff:2 * ff, :], x, (1, 0)).astype(BF16)
    down_grad[...] = dot(turned[2 * ff:, :], dy, (1, 0)).astype(BF16)
    token_grad[...] = dot(pick_ref[...], sg_ref[...], (0, 0)).astype(BF16)


def grads(ids, logits, score, slot_grad, act, xdy, width):
    slots = act.shape[0]
    ff = act.shape[1] // 3
    rows = ids.shape[1]
    tile = 512 if width % 512 == 0 else 256
    tiles = width // tile

    def whole(shape):
        return pl.BlockSpec(shape, lambda i: (0, 0))

    def column(height, shift=0):
        return pl.BlockSpec((height, tile), lambda i: (0, i + shift))

    return pl.pallas_call(
        grads_kernel,
        grid=(tiles,),
        out_shape=(
            jax.ShapeDtypeStruct((rows, width), BF16),
            jax.ShapeDtypeStruct((2, rows), F32),
            jax.ShapeDtypeStruct((ff, width), BF16),
            jax.ShapeDtypeStruct((ff, width), BF16),
            jax.ShapeDtypeStruct((ff, width), BF16),
        ),
        in_specs=[
            whole((2, rows)),
            whole((2, rows)),
            whole((CAP, LANES)),
            column(CAP),
            whole((slots, 3 * ff)),
            column(slots),
            column(slots, tiles),
        ],
        out_specs=(column(rows), whole((2, rows)), column(ff), column(ff), column(ff)),
        scratch_shapes=[pltpu.VMEM((3 * ff, slots), BF16), pltpu.VMEM((CAP, rows), BF16)],
        compiler_params=pltpu.CompilerParams(vmem_limit_bytes=60 * 1024 * 1024),
    )(ids, logits, score, slot_grad, act, xdy, xdy)


def solution(mesh):
    n, n_exp = mesh.shape["ctx"], mesh.shape["exp"]

    def shards(tokens, cotangent, route_logits, expert_ids, w_gate, w_up, w_down):
        ids, logits = expert_ids.T, route_logits.T
        xdy, act, slot_grad, score = exchange(
            n, n_exp, ids, logits, tokens, cotangent, w_gate, w_up, w_down
        )
        token_grad, logit_grad, gate_grad, up_grad, down_grad = grads(
            ids, logits, score, slot_grad, act, xdy, tokens.shape[1]
        )
        return token_grad, logit_grad.T, gate_grad, up_grad, down_grad

    features = P(("groups", "ctx", "tp"), "exp")
    routes = P(("groups", "ctx", "tp"), None)
    weights = P(("ctx", "tp"), "exp")
    return jax.shard_map(
        shards,
        mesh=mesh,
        in_specs=(features, features, routes, routes, weights, weights, weights),
        out_specs=(features, routes, features, features, features),
        check_vma=False,
    )
```

time: 276 us -> 84.4 us (0.31)
  waiting for transfers between devices: 145 us -> 0 us
  Pallas kernels: 0 us -> 83.4 us
  matrix products: 39.9 us -> 0 us
  blocking collectives: 30.1 us -> 0 us
  other arithmetic: 29.6 us -> 0 us
  local copies, waits for them, and re-layouts: 15.1 us -> 0 us
  between operations: 15.2 us -> 0.64 us
    pallas_call x0 -> x2, Pallas kernels: none -> 83.4 us  [the longest x1 72.9 us: exchange(): pl.pallas_call(functools.partial(exchange_kernel, n, n_exp), out_shape=(j...]
    psum x1 -> x0, waiting for transfers between devices: 83.3 us -> none  [shards(): lax.psum((partials[0], partials[1], partials[2]), 'exp')]
    dot_general x8 -> x0, matrix products: 39.9 us -> none  [the longest x3 17.9 us: contract_rows(): lax.dot_general(left, right, (((1,), (1,)), ((), ())), preferred_element_...]
    all_gather x2 -> x0, waiting for transfers between devices: 38.7 us -> none  [the longest x1 23.7 us: shards(): lax.all_gather(x_send, ('ctx', 'tp'), axis=0, tiled=True)]
    unnamed x2 -> x0, blocking collectives: 30.1 us -> none
    reduce_scatter x1 -> x0, waiting for transfers between devices: 23.4 us -> none  [shards(): lax.psum_scatter(jnp.dot(gate_back, w_gate, preferred_element_type=jnp.fl...]
    select_n x3 -> x0, other arithmetic: 21.4 us -> none  [the longest x1 20.1 us: shards(): token_score = jnp.where(chosen, own_score[source_row], 0.0)]
    scatter x3 -> x0, local copies, waits for them, and re-layouts: 10.4 us -> none  [the longest x2 8.2 us: shards(): jnp.zeros((CAP, feature_part), jnp.bfloat16).at[target]]
  transfers between devices with their start and end apart: 4 -> 0, of which waited for: 4 -> 0; matrix products, arithmetic and copies ran while one was open for 11% -> 0% of each run, Pallas kernels for 0% -> 0%
where the time goes in v1:
time: 84.4 us; the launch traced here: 84.1 us
  Pallas kernels  83.4 us (99%)
    pallas_call x1, Pallas kernels, exchange(): pl.pallas_call(functools.partial(exchange_kernel, n, n_exp), out_shape=(j...  72.9 us
    pallas_call x1, Pallas kernels, grads(): pl.pallas_call(grads_kernel, grid=(tiles,), out_shape=(jax.ShapeDtypeStru...  10.6 us

profile of v1, /device:TPU:0, one launch (start us, length us, event | category | flops | bytes accessed | tf_op | source)
XLA Modules:
  0.0 84.1 jit_solution(1443906975796057662)
XLA Ops:
  0.6 72.9 %shard_map.110 = (bf16[256,6272]{1,0:T(8,128)(2,1)}, bf16[256,3072]{1,0:T(8,128)(2,1)}, bf16[32,3072]{1,0:T(8,128)(2,1)}, f32[32,128]{1,0:T(8,128)}) custom-call(s32[2,256]{1,0:T(2,128)} %bitcast.3, f32[2,256]{1,0:T(2,128)} %bitcast.5, bf16[256,3072]{1,0:T(8,128)(2,1)} %tok_hbm.1, bf16[256,3072]{1,0:T(8,128)(2,1)} %cot_hbm.1, bf16[1024,3072]{1,0:T(8,128)(2,1)} %wg_hbm.1, ...), custom_call_target="tpu_custom_call" | custom-call | tf_op jit(solution)/shard_map/pallas_call | solution.py:335
  73.5 10.6 %shard_map.111 = (bf16[256,3072]{1,0:T(8,128)(2,1)}, f32[2,256]{1,0:T(2,128)}, bf16[1024,3072]{1,0:T(8,128)(2,1)}, bf16[1024,3072]{1,0:T(8,128)(2,1)}, bf16[1024,3072]{1,0:T(8,128)(2,1)}) custom-call(s32[2,256]{1,0:T(2,128)} %bitcast.4, f32[2,256]{1,0:T(2,128)} %bitcast.6, f32[32,128]{1,0:T(8,128)} %get-tuple-element.14.score_ref, ...), custom_call_target="tpu_custom_call" | custom-call | tf_op jit(solution)/shard_map/pallas_call | solution.py:420

commit v2 on v1

--- a/solution.py
+++ b/solution.py
@@ -48,7 +48,7 @@
     n, n_exp,
     ids_ref, logits_ref, tok_hbm, cot_hbm, wg_hbm, wu_hbm, wd_hbm,
     xdy_out, act_out, sg_ref, score_ref,
-    tok, cot, wg, wu, wd, xdy, part, psend, precv, act, grad, sib_out, sib_in, rs_out, rs_in, acc,
+    tok, cot, wg, wu, wd, xdy, psend, precv, act, grad, sib_out, sib_in, rs_out, rs_in, acc,
     load_sem, ag_send, ag_recv, sib_send, sib_recv, x_send, x_recv,
     gs_send, gs_recv, rs_send, rs_recv, xo_sem, ao_sem,
 ):
@@ -180,15 +180,23 @@
 
     def forward(k):
         j = nth(k)
-        paired = k <= 2 * both
-
-        @pl.when((k > 0) & jnp.logical_not(paired & (k % 2 == 0)))
+        second = (k >= 2) & (k % 2 == 0) & (k <= 2 * both)
+
+        @pl.when((k == 1) | ((k > 2 * both) & (k >= 2) & (k != 2 * both + 1)))
         def _():
             arrive(j)
 
-        @pl.when((k % 2 == 1) & (k + 1 <= 2 * both))
+        @pl.when((k == 1) & (2 <= 2 * both))
         def _():
             arrive(nth(k + 1))
+
+        @pl.when(second & (k + 1 < n))
+        def _():
+            arrive(nth(k + 1))
+
+        @pl.when(second & (k + 2 <= 2 * both))
+        def _():
+            arrive(nth(k + 2))
 
         twin_copy(j, sib).wait_recv()
         xdy_store(j).start()
@@ -201,7 +209,6 @@
             block = xdy[rows, first:first + width]
             for at in range(0, ff, ff_tile):
                 out = dot(block, weight[at:at + ff_tile, :], (1, 1))
-                part[i, rows, at:at + ff_tile] = out
                 psend[i, rows, at:at + ff_tile] = out.astype(BF16)
             for step in range(1, n_exp):
                 partial_copy(j, i, step).start()
@@ -218,7 +225,7 @@
         for at in range(0, ff, ff_tile):
             sums = []
             for i in range(3):
-                total = part[i, rows, at:at + ff_tile]
+                total = psend[i, rows, at:at + ff_tile].astype(F32)
                 for step in range(1, n_exp):
                     total = total + precv[step - 1, i, rows, at:at + ff_tile].astype(F32)
                 sums.append(total)
@@ -272,19 +279,19 @@
             rs_out[j, :, width + LANES:] = low
             home_copy(j, c).start()
 
-    @pl.loop(0, n)
+    @pl.loop(0, n + 2)
     def _(k):
-        forward(k)
-
-    @pl.loop(0, n + 1)
-    def _(k):
-        @pl.when(k >= 1)
-        def _():
-            finish(k - 1)
-
         @pl.when(k < n)
         def _():
-            backward(k)
+            forward(k)
+
+        @pl.when(k >= 2)
+        def _():
+            finish(k - 2)
+
+        @pl.when((k >= 1) & (k <= n))
+        def _():
+            backward(k - 1)
 
     @pl.loop(0, n)
     def _(j):
@@ -349,7 +356,6 @@
             pltpu.VMEM((ff, width), BF16),
             pltpu.VMEM((ff, width), BF16),
             pltpu.VMEM((slots, wide), BF16),
-            pltpu.VMEM((3, slots, ff), F32),
             pltpu.VMEM((3, slots, ff), BF16),
             pltpu.VMEM((n_exp - 1, 3, slots, ff), BF16),
             pltpu.VMEM((slots, 3 * ff), BF16),
@@ -408,7 +414,7 @@
     slots = act.shape[0]
     ff = act.shape[1] // 3
     rows = ids.shape[1]
-    tile = 512 if width % 512 == 0 else 256
+    tile = 256
     tiles = width // tile
 
     def whole(shape):

time: 84.4 us -> 82.1 us (0.973)
  Pallas kernels: 83.4 us -> 81 us
    pallas_call x1, Pallas kernels: 72.9 us -> 66.5 us  [exchange(): pl.pallas_call(functools.partial(exchange_kernel, n, n_exp), out_shape=(j...]
    pallas_call x1, Pallas kernels: 10.6 us -> 14.4 us  [grads(): pl.pallas_call(grads_kernel, grid=(tiles,), out_shape=(jax.ShapeDtypeStru...]
where the time goes in v2:
time: 82.1 us; the launch traced here: 81.6 us
  Pallas kernels  81 us (99%)
    pallas_call x1, Pallas kernels, exchange(): pl.pallas_call(functools.partial(exchange_kernel, n, n_exp), out_shape=(j...  66.5 us
    pallas_call x1, Pallas kernels, grads(): pl.pallas_call(grads_kernel, grid=(tiles,), out_shape=(jax.ShapeDtypeStru...  14.4 us

profile of v2, /device:TPU:0, one launch (start us, length us, event | category | flops | bytes accessed | tf_op | source)
XLA Modules:
  0.0 81.6 jit_solution(12401236410317717859)
XLA Ops:
  0.6 66.5 %shard_map.110 = (bf16[256,6272]{1,0:T(8,128)(2,1)}, bf16[256,3072]{1,0:T(8,128)(2,1)}, bf16[32,3072]{1,0:T(8,128)(2,1)}, f32[32,128]{1,0:T(8,128)}) custom-call(s32[2,256]{1,0:T(2,128)} %bitcast.3, f32[2,256]{1,0:T(2,128)} %bitcast.5, bf16[256,3072]{1,0:T(8,128)(2,1)} %tok_hbm.1, bf16[256,3072]{1,0:T(8,128)(2,1)} %cot_hbm.1, bf16[1024,3072]{1,0:T(8,128)(2,1)} %wg_hbm.1, ...), custom_call_target="tpu_custom_call" | custom-call | tf_op jit(solution)/shard_map/pallas_call | solution.py:342
  67.2 14.4 %shard_map.111 = (bf16[256,3072]{1,0:T(8,128)(2,1)}, f32[2,256]{1,0:T(2,128)}, bf16[1024,3072]{1,0:T(8,128)(2,1)}, bf16[1024,3072]{1,0:T(8,128)(2,1)}, bf16[1024,3072]{1,0:T(8,128)(2,1)}) custom-call(s32[2,256]{1,0:T(2,128)} %bitcast.4, f32[2,256]{1,0:T(2,128)} %bitcast.6, f32[32,128]{1,0:T(8,128)} %get-tuple-element.14.score_ref, ...), custom_call_target="tpu_custom_call" | custom-call | tf_op jit(solution)/shard_map/pallas_call | solution.py:426
